TPU v7x, 256 devices: a whole 4x4x8 slice. The times are simulated.
256 devices in a mesh: ctx: 64 (over z, x, core), head: 4 (over y).
Axes of the slice: x: 4, y: 4, z: 8, core: 2. Of those that a mesh axis runs over, the one named last changes fastest.
Arguments:
- query_plain: bfloat16 [4096, 64, 128], P('ctx', 'head'), may hold values from -6 to 6
- query_rotary: bfloat16 [4096, 64, 64], P('ctx', 'head'), may hold values from -480 to 480
- latent_cache: bfloat16 [4096, 512], P('ctx'), may hold values from -6 to 6
- key_rotary: bfloat16 [4096, 64], P('ctx'), may hold values from -4 to 4
- latent_gain: float32 [512], replicated, may hold values from 0.1 to 1.9
- positions: int32 [4096], P('ctx'), may hold values from 0 to 4095, as said below
- absorb_keys: bfloat16 [64, 128, 512], P('head'), may hold values from -0.5 to 0.5
- absorb_values: bfloat16 [64, 512, 128], P('head'), may hold values from -0.25 to 0.25
- output_weight: bfloat16 [64, 128, 3584], P('head', 'ctx'), may hold values from -0.0625 to 0.0625
Outputs:
- attention_out: bfloat16 [4096, 3584], P('ctx', 'head')
Inputs may be any that keep to these rules, and one draw needn't show every extreme that they name: A permutation of the 4096 positions; the stored tokens come in aligned blocks of 32 rows, each block holding 32 consecutive positions in ascending order; the blocks stand in any order.
All inputs are finite; a program needn't handle non-finite values.
Results may differ from a plain program's by a relative error of at most 0.018.
The roundings to bfloat16 on the way count: a program that leaves them out, or rounds other values in their place, can miss the bound.
Values may be sent and summed in bfloat16 or wider, within the bound.
A program may use at most 128 MiB of HBM per device.

v0:
```python
import math

import jax
import jax.numpy as jnp
from jax import lax
from jax.sharding import PartitionSpec as P

norm_epsilon = 1e-06
rope_base = 10000.0
masked_score = -1e30


def rotate(values, where_at):
    half_width = values.shape[-1] // 2
    frequency = rope_base ** (-jnp.arange(half_width, dtype=jnp.float32) / half_width)
    angles = where_at.astype(jnp.float32)[..., None] * frequency
    cosine_part = jnp.cos(angles)
    sine_part = jnp.sin(angles)
    first_half = values[..., :half_width]
    second_half = values[..., half_width:]
    return jnp.concatenate(
        [
            first_half * cosine_part - second_half * sine_part,
            second_half * cosine_part + first_half * sine_part,
        ],
        axis=-1,
    )


def body(
    query_plain,
    query_rotary,
    latent_cache,
    key_rotary,
    latent_gain,
    positions,
    absorb_keys,
    absorb_values,
    output_weight,
):
    local_tokens = query_plain.shape[0]
    local_heads = query_plain.shape[1]
    latent_width = latent_cache.shape[1]
    score_scale = (absorb_keys.shape[1] + key_rotary.shape[1]) ** (-0.5)
    raw_latent = latent_cache.astype(jnp.float32)
    latent = (
        raw_latent
        * lax.rsqrt(jnp.mean(raw_latent * raw_latent, axis=-1, keepdims=True) + norm_epsilon)
        * latent_gain
    ).astype(jnp.bfloat16)
    key_rot = rotate(key_rotary.astype(jnp.float32), positions).astype(jnp.bfloat16)
    keys = jnp.concatenate([latent, key_rot], axis=-1)
    query_abs = jnp.einsum(
        "thn,hnl->thl", query_plain, absorb_keys, preferred_element_type=jnp.float32
    ).astype(jnp.bfloat16)
    query_rot = rotate(query_rotary.astype(jnp.float32), positions[:, None]).astype(jnp.bfloat16)
    queries = jnp.concatenate([query_abs, query_rot], axis=-1).reshape(
        local_tokens * local_heads, -1
    )
    query_pos = jnp.broadcast_to(positions[:, None], (local_tokens, local_heads)).reshape(-1)
    query_rows = local_tokens * local_heads

    def update(running, block_keys, block_pos):
        top_score, weight_sum, context_sum = running
        scores = (
            lax.dot_general(
                queries, block_keys, (((1,), (1,)), ((), ())), preferred_element_type=jnp.float32
            )
            * score_scale
        )
        visible = block_pos[None, :] <= query_pos[:, None]
        masked = jnp.where(visible, scores, masked_score)
        new_top = jnp.maximum(top_score, jnp.max(masked, axis=1))
        expo = jnp.where(visible, jnp.exp(masked - new_top[:, None]), 0.0)
        shrink = jnp.exp(top_score - new_top)
        weight_sum = weight_sum * shrink + jnp.sum(expo, axis=1)
        context_sum = context_sum * shrink[:, None] + jnp.dot(
            expo.astype(jnp.bfloat16),
            block_keys[:, :latent_width],
            preferred_element_type=jnp.float32,
        )
        return (new_top, weight_sum, context_sum)

    start_state = (
        jnp.full((query_rows,), masked_score, jnp.float32),
        jnp.zeros((query_rows,), jnp.float32),
        jnp.zeros((query_rows, latent_width), jnp.float32),
    )
    running = start_state
    piece_keys = lax.all_gather(keys, "ctx", axis=0, tiled=True)
    piece_pos = lax.all_gather(positions, "ctx", axis=0, tiled=True)
    block_rows = piece_keys.shape[0]
    block_size = math.gcd(block_rows, 512)
    block_count = block_rows // block_size
    stacked_keys = piece_keys.reshape(block_count, block_size, piece_keys.shape[1])
    stacked_pos = piece_pos.reshape(block_count, block_size)

    def step(state, inputs):
        block_keys, block_pos = inputs
        state = update(state, block_keys, block_pos)
        return (state, None)

    running, unused = lax.scan(step, running, (stacked_keys, stacked_pos))
    top_score, weight_sum, context_sum = running
    context = (
        (context_sum / weight_sum[:, None])
        .astype(jnp.bfloat16)
        .reshape(local_tokens, local_heads, latent_width)
    )
    head_out = jnp.einsum(
        "thl,hlv->thv", context, absorb_values, preferred_element_type=jnp.float32
    ).astype(jnp.bfloat16)
    partial_out = jnp.einsum(
        "thv,hvd->td",
        head_out,
        lax.all_gather(output_weight, "ctx", axis=1, tiled=True),
        preferred_element_type=jnp.float32,
    )
    return lax.psum_scatter(
        partial_out.astype(jnp.bfloat16), "head", scatter_dimension=1, tiled=True
    )


def solution(mesh):
    return jax.shard_map(
        body,
        mesh=mesh,
        in_specs=(
            P("ctx", "head", None),
            P("ctx", "head", None),
            P("ctx", None),
            P("ctx", None),
            P(),
            P("ctx"),
            P("head", None, None),
            P("head", None, None),
            P("head", "ctx", None),
        ),
        out_specs=P("ctx", "head"),
        check_vma=False,
    )
```

profile of v0, /device:TPU:2, one launch (start us, length us, event | category | flops | bytes accessed | tf_op | source)
XLA Modules:
  0.0 416.7 jit_solution(2970963350825897763)
XLA Ops:
  6.6 0.9 convert_element_type.42
  7.4 0.7 convert_element_type.43
  8.1 1.0 fusion.31
  9.1 0.9 fusion.33
  10.2 0.7 pad_maximum_fusion.1
  11.0 1.7 copy.19
  12.8 1.0 copy_convert_fusion
  14.8 1.9 copy.17
  16.6 0.6 dynamic-slice
  18.2 249.9 %all-reduce = s32[4096]{0:T(1024)S(1)} all-reduce(s32[4096]{0:T(1024)S(1)} %dynamic-update-slice), channel_id=1, replica_groups=mesh['ctx'=64,'head'=4] {'ctx'}, use_global_device_ids=true, to_apply=%add | all-reduce | flops 4096 | bytes 32768
  268.0 90.0 %while.15 = (s32[]{:T(128)}, f32[1024]{0:T(1024)S(1)}, f32[1024]{0:T(1024)S(1)}, f32[1024,512]{1,0:T(8,128)}, s32[8,512]{1,0:T(8,128)S(1)}, /*index=5*/bf16[8,51...) while((s32[]{:T(128)}, f32[1024]{0:T(1024)S(1)}, ...), condition=%wide.region_4.5_spmd.clone, body=%wide.region_1.4_spmd.clone.sunk | while | flops 1150817280 | bytes 22448532 | solution.py:103
  268.1 1.2 dynamic-slice_bitcast_fusion.2
  269.4 3.7 fusion.50
  273.1 2.4 fusion.51
  275.5 2.4 fusion.53
  277.9 1.2 dynamic-slice_bitcast_fusion.2
  279.2 3.7 fusion.50
  283.0 2.4 fusion.51
  285.3 4.0 fusion.53
  289.4 1.2 dynamic-slice_bitcast_fusion.2
  290.7 3.7 fusion.50
  294.4 2.4 fusion.51
  296.8 4.0 fusion.53
  300.8 1.2 dynamic-slice_bitcast_fusion.2
  302.1 3.7 fusion.50
  305.8 2.4 fusion.51
  308.2 4.0 fusion.53
  312.2 1.2 dynamic-slice_bitcast_fusion.2
  313.6 3.7 fusion.50
  317.3 2.4 fusion.51
  319.7 4.0 fusion.53
  323.7 1.2 dynamic-slice_bitcast_fusion.2
  325.0 3.7 fusion.50
  328.7 2.4 fusion.51
  331.1 4.0 fusion.53
  335.1 1.2 dynamic-slice_bitcast_fusion.2
  336.4 3.7 fusion.50
  340.2 2.4 fusion.51
  342.6 4.0 fusion.53
  346.6 1.2 dynamic-slice_bitcast_fusion.2
  347.9 3.7 fusion.50
  351.6 2.4 fusion.51
  354.0 4.0 fusion.53
  358.0 1.8 divide_convert_fusion
  359.9 20.7 %fusion.23 = bf16[64,3584]{1,0:T(8,128)(2,1)} fusion(bf16[16,128,3584]{2,0,1:T(8,128)(2,1)} %all-gather.5.cloned.1.call-done, bf16[16,512,128]{2,1,0:T(8,128)(2,1)} %param.18, bf16[64,16,512]{2,1,0:T(8,128)(2,1)S(1)} %bitcast.51), kind=kOutput, calls=%fused_computation.27 | convolution fusion | flops 1074102272 | bytes 18284544 | tf_op jit(solution)/shard_map/thv,hvd->td/dot_general | solution.py:113
  380.5 2.3 copy.21
  382.8 25.7 %reduce-scatter.4.cloned.1.call-done = bf16[896,64]{1,0:T(8,128)(2,1)} async-done(((bf16[3584,64]{1,0:T(8,128)(2,1)}), bf16[896,64]{1,0:T(8,128)(2,1)}) %reduce-scatter.4.cloned.1.call-update) | async-done | bytes 114704
  408.5 1.7 copy.22
  (92 shorter events, 3.0 us)
Async XLA Ops:
  6.5 7.5 %copy-start = (bf16[16,128,512]{2,1,0:T(8,128)(2,1)S(1)}, bf16[16,128,512]{2,1,0:T(8,128)(2,1)}, u32[]{:S(2)}) copy-start(bf16[16,128,512]{2,1,0:T(8,128)(2,1)} %param.17) | copy-start | bytes 6291460
  6.5 7.5 %copy-start.2 = (bf16[64,16,128]{2,1,0:T(8,128)(2,1)S(1)}, bf16[64,16,128]{2,1,0:T(8,128)(2,1)}, u32[]{:S(2)}) copy-start(bf16[64,16,128]{2,1,0:T(8,128)(2,1)} %param.11) | copy-start | bytes 786436
  6.5 261.5 %all-gather.3.cloned.1.call-start = ((), (), s32[]{:S(2)}) async-start(), calls=%async_computation.1 | async-start | bytes 5324800 | tf_op jit(solution)/shard_map/all_gather | solution.py:90
  10.9 348.9 %all-gather.5.cloned.1.call-start = ((), (), s32[]{:S(2)}) async-start(), calls=%async_computation.2 | async-start | bytes 14909440 | tf_op jit(solution)/shard_map/all_gather | solution.py:116
  12.7 395.8 %reduce-scatter.4.cloned.1.call-start = ((), (), s32[]{:S(2)}) async-start(), calls=%async_computation.3 | async-start | bytes 1146880
  14.5 2.1 copy-start.4
  14.5 3.4 copy-start.3
  273.1 2.4 copy-start.1
  283.0 2.4 copy-start.1
  294.4 2.4 copy-start.1
  305.8 2.4 copy-start.1
  317.3 2.4 copy-start.1
  328.7 2.4 copy-start.1
  340.2 2.4 copy-start.1
  351.6 2.4 copy-start.1
Sparse Core Ops, SparseCore 0:
  11.1 81.6 all-gather.2
  95.5 91.7 all-gather.4
  382.9 25.5 reduce-scatter.3
where the time goes:
time: 418 us; the launch traced here: 417 us
  blocking collectives  250 us (60%)
  matrix products  81.4 us (19%)
  other arithmetic  26.6 us (6%)
  waiting for transfers between devices  25.8 us (6%)
  local copies, waits for them, and re-layouts  18.9 us (5%)
  between operations  13.9 us (3%)
    unnamed x1, blocking collectives  250 us
    dot_general x8, matrix products, update(): jnp.dot(expo.astype(jnp.bfloat16), block_keys[:, :latent_width], preferre...  30.4 us
    dot_general x8, matrix products, update(): lax.dot_general(queries, block_keys, (((1,), (1,)), ((), ())), preferred_...  29.9 us
    unnamed x4, waiting for transfers between devices  25.7 us
    dot_general x1, matrix products, body(): jnp.einsum('thv,hvd->td', head_out, lax.all_gather(output_weight, 'ctx',...  20.7 us
    reduce_sum x8, other arithmetic, update(): weight_sum = weight_sum * shrink + jnp.sum(expo, axis=1)  18.8 us
    squeeze x8, local copies, waits for them, and re-layouts, body(): running, unused = lax.scan(step, running, (stacked_keys, stacked_pos))  9.21 us
  transfers between devices with their start and end apart: 3, of which 1 were waited for; matrix products, arithmetic and copies ran while one was open for 23% of the time, Pallas kernels for 0%

commit v1 on v0

v1 whole, which is shorter than its diff:
```python
import jax
import jax.numpy as jnp
from jax import lax
from jax.experimental import pallas as pl
from jax.experimental.pallas import tpu as pltpu
from jax.sharding import PartitionSpec as P

MESH = pl.DeviceIdType.MESH
norm_epsilon = 1e-06
rope_base = 10000.0
masked_score = -1e30

NZ, NX, NY = 8, 4, 4
TOK = 64
HALF = 32
HEADS = 16
ROWS = TOK * HEADS
NOPE, ROPE, LAT, VD = 128, 64, 512, 128
COLS = 896
CHUNK = 256
CHUNKS = ROWS // CHUNK
WIDE = 2 * LAT + 2 * ROPE
SCALE = 192 ** (-0.5)
LOG2E = 1.4426950408889634

SLOTS = [
    "own", "R1", "L1", "Dm0", "Dp0", "R2", "L2", "Do0",
    "R3", "L3", "Ym", "Yp", "R4", "Yo", "Dm3", "Dp3",
    "Em", "Ep", "Amm", "Apm", "Amp", "App", "Amo", "Apo",
    "Fm", "Fp", "Do3", "Eo", "Aom", "Aop", "Aoo", "Fo",
]
SLOT = {name: i for i, name in enumerate(SLOTS)}

FORWARD = {
    "own": [("z+", "R1"), ("z-", "L1"), ("x+", "Dm0"), ("x-", "Dp0")],
    "R1": [("z+", "R2")],
    "R2": [("z+", "R3")],
    "R3": [("z+", "R4"), ("x+", "Dm3"), ("x-", "Dp3")],
    "L1": [("z-", "L2")],
    "L2": [("z-", "L3")],
    "L3": [("x+", "Em"), ("x-", "Ep")],
    "R4": [("x+", "Fm"), ("x-", "Fp")],
    "Dm0": [("x+", "Do0")],
    "Dp3": [("x-", "Do3")],
    "Em": [("x+", "Eo")],
    "Fp": [("x-", "Fo")],
    "Ym": [("x+", "Yo"), ("y+", "Amm"), ("y-", "Apm")],
    "Yp": [("y+", "Amp"), ("y-", "App")],
    "Yo": [("y+", "Amo"), ("y-", "Apo")],
    "Amm": [("y+", "Aom")],
    "App": [("y-", "Aop")],
    "Amo": [("y+", "Aoo")],
}
SHARED = {"R1": 0, "L1": 1, "R2": 2, "L2": 3}

XD = {"m": 3, "p": 1, "o": 2}


def origin(name):
    if name == "own":
        return 0, 0
    if name[0] == "R":
        return 0, NZ - int(name[1])
    if name[0] == "L":
        return 0, int(name[1])
    if name[0] == "D":
        return XD[name[1]], (0 if name[2] == "0" else NZ - 3)
    if name[0] == "E":
        return XD[name[1]], 3
    if name[0] == "F":
        return XD[name[1]], 4
    if name[0] == "Y":
        return XD[name[1]], ("y", 0)
    return XD[name[2]], ("y", XD[name[1]])


def kernel(
    qp_ref, qr_ref, lat_ref, kr_ref, gain_ref, pos_ref, cos_ref, sin_ref, ak_hbm, av_hbm, w_ref,
    out_ref,
    ak, av, kx, qh, q2, s_buf, top, kpos, psrc, pline, pall, wp, wf, ctx_acc, ho, acc, outs, rcv,
    local_sem, key_send, key_recv, sib_send, sib_recv, p_send, p_recv, w1_send, w1_recv,
    w2_send, w2_recv, w3_send, w3_recv, ho_send, ho_recv, out_send, out_recv,
):
    f32, bf16 = jnp.float32, jnp.bfloat16
    me = lax.axis_index("ctx")
    y = lax.axis_index("head")
    core = lax.rem(me, 2)
    x = lax.rem(me // 2, NX)
    z = me // (2 * NX)

    def device(dz=0, dx=0, dc=0, dy=0):
        nz = lax.rem(z + (dz + NZ), NZ)
        nx = lax.rem(x + (dx + NX), NX)
        nc = lax.rem(core + dc, 2)
        ny = lax.rem(y + (dy + NY), NY)
        return ((nz * NX + nx) * 2 + nc, ny)

    sibling = device(dc=1)
    where = {
        "z+": device(dz=1), "z-": device(dz=-1), "x+": device(dx=1), "x-": device(dx=-1),
        "y+": device(dy=1), "y-": device(dy=-1),
    }
    column_peers = [device(dz=d) for d in range(1, NZ)]
    chip_peers = [(dx, dc) for dx in range(NX) for dc in range(2) if (dx, dc) != (0, 0)]
    plane_peers = [device(dx=dx, dy=dy) for dx in range(NX) for dy in range(1, NY)]
    partners = column_peers + [device(dx=a, dc=b) for a, b in chip_peers] + plane_peers

    barrier = pltpu.get_barrier_semaphore()
    for partner in partners:
        pl.semaphore_signal(barrier, inc=1, device_id=partner, device_id_type=MESH)

    load_ak = pltpu.make_async_copy(ak_hbm, ak, local_sem.at[0])
    load_av = pltpu.make_async_copy(av_hbm, av, local_sem.at[1])
    load_ak.start()
    load_av.start()

    def remote(src, dst, send, recv, to):
        return pltpu.make_async_remote_copy(
            src_ref=src, dst_ref=dst, send_sem=send, recv_sem=recv, device_id=to, device_id_type=MESH
        )

    def dot(a, b):
        return jnp.dot(a, b, preferred_element_type=f32)

    def iota(shape, axis):
        return lax.broadcasted_iota(jnp.int32, shape, axis)

    def onehot(mask):
        return jnp.where(mask, 1.0, 0.0).astype(bf16)

    def slot_ref(p, sib=0):
        return kx.at[2 * (p // 8) + sib, pl.ds((p % 8) * HALF, HALF), :]

    pending = []

    def send_block(p, to, dst):
        index = len(pending)
        copy = remote(slot_ref(p), slot_ref(dst), key_send.at[index], key_recv.at[dst], to)
        copy.start()
        pending.append(copy)

    def to_sibling(p):
        remote(slot_ref(p), slot_ref(p, 1), sib_send.at[p], sib_recv.at[p], sibling).start()

    def filled(name):
        p = SLOT[name]
        for direction, dst in FORWARD.get(name, []):
            send_block(p, where[direction], SLOT[dst])
        to_sibling(p)
        if name in SHARED:

            @pl.when(y == SHARED[name])
            def _():
                for k, (direction, dst) in enumerate((("x+", "Ym"), ("x-", "Yp"))):
                    remote(
                        slot_ref(p), slot_ref(SLOT[dst]), key_send.at[60 + k],
                        key_recv.at[SLOT[dst]], where[direction],
                    ).start()

    def arrived(name):
        p = SLOT[name]
        remote(slot_ref(p), slot_ref(p), key_send.at[0], key_recv.at[p], sibling).wait_recv()
        filled(name)

    raw = lat_ref[...].astype(f32)
    spread = jnp.sum(raw * raw, axis=-1, keepdims=True) * (1.0 / LAT)
    latent = (raw * lax.rsqrt(spread + norm_epsilon) * gain_ref[...]).astype(bf16)
    row_i, col_i = iota((ROPE, 128), 0), iota((ROPE, 128), 1)
    low = iota((HALF, 128), 1) < ROPE
    kr = kr_ref[...]
    first = onehot(col_i == row_i)
    second = onehot(col_i == row_i + ROPE)
    turned = (row_i + HALF) & (ROPE - 1)
    first_turned = onehot(col_i == turned)
    second_turned = onehot(col_i == turned + ROPE)
    straight = dot(kr[:HALF], first) + dot(kr[HALF:], second)
    crossed = dot(kr[:HALF], first_turned) + dot(kr[HALF:], second_turned)
    cosine, sine = cos_ref[...], sin_ref[...]
    key_rot = straight * jnp.where(low, cosine[:HALF], cosine[HALF:]) + crossed * jnp.where(
        low, sine[:HALF], sine[HALF:]
    )
    kx[0, 0:HALF, 0:LAT] = latent[:HALF]
    kx[0, 0:HALF, LAT : LAT + 128] = key_rot.astype(bf16)
    kx[0, 0:HALF, LAT + 128 : WIDE] = latent[HALF:]
    lane = iota((8, 2 * CHUNK), 1)
    base = jnp.where(lane < CHUNK, pos_ref[0:1, 0:1], pos_ref[HALF : HALF + 1, 0:1])
    psrc[...] = base + (lane & (HALF - 1)).astype(f32)

    pl.semaphore_wait(barrier, len(partners))

    filled("own")
    column_sends = []
    for d in range(1, NZ):
        copy = remote(psrc, pline.at[NZ - d], p_send.at[d], p_recv.at[NZ - d], column_peers[d - 1])
        copy.start()
        column_sends.append(copy)

    def weight_piece(nx, nc):
        return w_ref.at[
            pl.ds(pl.multiple_of(nc * 16, 16), 16), pl.ds(pl.multiple_of(nx * COLS, 128), COLS)
        ]

    my_place = x * 2 + core
    weight_sends = []
    for k, (dx, dc) in enumerate(chip_peers):
        nx, nc = lax.rem(x + dx, NX), lax.rem(core + dc, 2)
        copy = remote(
            weight_piece(nx, nc), wp.at[my_place], w1_send.at[k], w1_recv.at[my_place],
            device(dx=dx, dc=dc),
        )
        copy.start()
        weight_sends.append(copy)
    own_weight = pltpu.make_async_copy(weight_piece(x, core), wp.at[my_place], local_sem.at[2])
    own_weight.start()

    big_i, big_j = iota((256, 256), 0), iota((256, 256), 1)
    swap = onehot(big_j == ((big_i & 15) << 4) + (big_i >> 4))
    doubled = jnp.concatenate(
        [first + second, first_turned + second_turned], axis=1
    )
    low_q = iota((256, 128), 1) < ROPE
    for b in range(TOK // 16):
        rows = slice(b * 256, (b + 1) * 256)
        plain = dot(swap, qp_ref[rows, :]).astype(bf16).reshape(HEADS, 16, NOPE)
        qh[:, b * 16 : (b + 1) * 16, :] = plain
        both = dot(swap, dot(qr_ref[rows, :], doubled).astype(bf16))
        tokens = slice(b * 16, (b + 1) * 16)
        c_rows = jnp.concatenate([cosine[tokens]] * HEADS, axis=0)
        s_rows = jnp.concatenate([sine[tokens]] * HEADS, axis=0)
        turned_q = both[:, :128] * c_rows + both[:, 128:] * s_rows
        q_first = jnp.where(low_q, turned_q, 0.0).astype(bf16).reshape(HEADS, 16, 128)
        q_second = jnp.where(low_q, 0.0, turned_q).astype(bf16).reshape(HEADS, 16, 128)
        q2[:, b * 16 : (b + 1) * 16, 0:128] = q_second
        q2[:, b * 16 : (b + 1) * 16, 128 + LAT :] = q_first

    arrived("R1")
    arrived("L1")
    arrived("Dm0")
    arrived("Dp0")
    load_ak.wait()

    def absorb(h, carry):
        q2[h, :, 128 : 128 + LAT] = dot(qh[h], ak[h]).astype(bf16)
        return carry

    lax.fori_loop(0, HEADS // 2, absorb, 0)
    arrived("R2")
    arrived("L2")
    arrived("Do0")
    lax.fori_loop(HEADS // 2, HEADS, absorb, 0)

    for d in range(1, NZ):
        remote(psrc, pline.at[d], p_send.at[d], p_recv.at[d], sibling).wait_recv()
    line = psrc[...]
    which = iota((8, 2 * CHUNK), 0)
    for d in range(1, NZ):
        line = jnp.where(which == d, pline[d], line)
    pall[0] = line
    line_sends = []
    for k, (dx, dc) in enumerate(chip_peers):
        there = ((NX - dx) % NX) * 2 + dc
        copy = remote(
            pall.at[0], pall.at[there], p_send.at[8 + k], p_recv.at[8 + there], device(dx=dx, dc=dc)
        )
        copy.start()
        line_sends.append(copy)

    arrived("R3")
    arrived("L3")
    arrived("Ym")
    arrived("Yp")
    for k, (dx, dc) in enumerate(chip_peers):
        here = dx * 2 + dc
        remote(pall.at[0], pall.at[here], p_send.at[0], p_recv.at[8 + here], sibling).wait_recv()

    def shared_offset(dy):
        owner = lax.rem(y + dy, NY)
        far, sign = 1 + owner // 2, lax.rem(owner, 2) * 2 - 1
        return lax.rem(far * sign + NZ, NZ)

    group = (iota((1, 2 * CHUNK), 1) & (CHUNK - 1)) >> 5
    for tile in range(8):
        stage, dc = tile // 2, tile % 2
        value = jnp.zeros((1, 2 * CHUNK), f32)
        for q in range(8):
            dx, dz = origin(SLOTS[stage * 8 + q])
            if isinstance(dz, tuple):
                dz = shared_offset(dz[1])
            value = jnp.where(group == q, pall[dx * 2 + dc, pl.ds(dz, 1), :], value)
        kpos[tile, 0:1, :] = value

    query_pos = jnp.concatenate([pos_ref[:, 0:1]] * (CHUNK // TOK), axis=0)
    top[...] = jnp.full(top.shape, masked_score, f32)
    contract = (((1,), (1,)), ((), ()))
    chunk_heads = CHUNK // TOK

    def scores(tile):
        def one(r, carry):
            heads = pl.ds(r * chunk_heads, chunk_heads)
            rows = pl.ds(pl.multiple_of(r * CHUNK, CHUNK), CHUNK)
            q_a = q2[heads, :, 128:].reshape(CHUNK, LAT + 128)
            q_b = q2[heads, :, 0 : LAT + 128].reshape(CHUNK, LAT + 128)
            best = top[rows, :]
            for part, (q, k) in enumerate(
                ((q_a, kx[tile, :, 0 : LAT + 128]), (q_b, kx[tile, :, LAT:WIDE]))
            ):
                s = lax.dot_general(q, k, contract, preferred_element_type=f32)
                lanes = slice(part * CHUNK, (part + 1) * CHUNK)
                s = jnp.where(kpos[tile, 0:1, lanes] <= query_pos, s, masked_score)
                s_buf[tile, rows, lanes] = s
                best = jnp.maximum(best, jnp.maximum(s[:, :128], s[:, 128:]))
            top[rows, :] = best
            return carry

        lax.fori_loop(0, CHUNKS, one, 0)

    def from_sibling(stage):
        for p in range(stage * 8, stage * 8 + 8):
            remote(
                slot_ref(p, 1), slot_ref(p, 1), sib_send.at[p], sib_recv.at[p], sibling
            ).wait_recv()

    scores(0)
    arrived("R4")
    arrived("Yo")

    for k, (dx, dc) in enumerate(chip_peers):
        place = lax.rem(x + dx, NX) * 2 + lax.rem(core + dc, 2)
        remote(wp.at[place], wp.at[place], w1_send.at[0], w1_recv.at[place], sibling).wait_recv()
    own_weight.wait()
    to_i, from_i = iota((128, 128), 0), iota((128, 128), 1)
    regroup = onehot(
        from_i == (((to_i & 15) >> 1) << 4) + ((to_i >> 4) << 1) + (to_i & 1)
    )
    share = dot(regroup, wp[...].reshape(128, COLS)).astype(bf16).reshape(8, 16, COLS)

    def weight_slot(dz, half):
        nz = lax.rem(z + (dz + NZ), NZ)
        return wf.at[
            pl.ds(core * 8 + half * 4, 4), pl.ds(pl.multiple_of(nz * 16, 16), 16), :
        ]

    wf[pl.ds(core * 8, 8), pl.ds(pl.multiple_of(z * 16, 16), 16), :] = share
    ring_sends = []

    def weight_on(dz, half):
        index = (dz % NZ) * 2 + half
        here = weight_slot(dz, half)
        copy = remote(here, here, w3_send.at[index], w3_recv.at[index], sibling)
        copy.start()
        ring_sends.append(copy)
        steps = []
        if -3 < dz <= 0 or (dz == -3 and half == 0):
            steps.append(("z+", dz - 1))
        if 0 <= dz < 3 or (dz == 3 and half == 1):
            steps.append(("z-", dz + 1))
        for direction, there in steps:
            arrival = (there % NZ) * 2 + half
            copy = remote(
                here, here, w2_send.at[len(ring_sends) - 1], w2_recv.at[arrival], where[direction]
            )
            copy.start()
            ring_sends.append(copy)

    def weight_arrived(dz, half):
        index = (dz % NZ) * 2 + half
        here = weight_slot(dz, half)
        remote(here, here, w2_send.at[0], w2_recv.at[index], sibling).wait_recv()
        weight_on(dz, half)

    def weight_step(step):
        for half in range(2):
            if step < 4:
                weight_arrived(-step, half)
                weight_arrived(step, half)
            else:
                weight_arrived(-4 if half == 0 else 4, half)

    weight_on(0, 0)
    weight_on(0, 1)

    arrived("Dm3")
    arrived("Dp3")
    from_sibling(0)
    scores(1)
    for name in SLOTS[16:20]:
        arrived(name)
    scores(2)
    for name in SLOTS[20:24]:
        arrived(name)
    from_sibling(1)
    scores(3)
    weight_step(1)
    for name in SLOTS[24:28]:
        arrived(name)
    scores(4)
    for name in SLOTS[28:32]:
        arrived(name)
    from_sibling(2)
    scores(5)
    scores(6)
    from_sibling(3)
    scores(7)
    weight_step(2)

    load_av.wait()
    factor = SCALE * LOG2E
    exchange = []

    def head_out_send(c, to, place, index):
        piece = ho.at[c, place]
        copy = remote(piece, piece, ho_send.at[index], ho_recv.at[index], to)
        copy.start()
        exchange.append(copy)

    def head_out_wait(c, dx):
        place = lax.rem(x + dx, NX)
        index = c * 3 + (dx - 1)
        piece = ho.at[c, place]
        remote(piece, piece, ho_send.at[0], ho_recv.at[index], sibling).wait_recv()
        return place

    def head_out_forward(c):
        place = head_out_wait(c, 3)
        if c % 2 == 0:
            head_out_send(c, where["x+"], place, c * 3 + 1)
        place = head_out_wait(c, 1)
        if c % 2 == 1:
            head_out_send(c, where["x-"], place, c * 3 + 1)

    for c in range(CHUNKS):
        rows = slice(c * CHUNK, (c + 1) * CHUNK)
        peak = jnp.max(top[rows, :], axis=1, keepdims=True)
        ctx_acc[...] = jnp.zeros(ctx_acc.shape, f32)

        def one(tile, total, rows=rows, peak=peak):
            grown = jnp.zeros((CHUNK, LAT), f32)
            for part, cols in enumerate((slice(0, LAT), slice(LAT + 128, WIDE))):
                lanes = slice(part * CHUNK, (part + 1) * CHUNK)
                expo = jnp.exp2((s_buf[tile, rows, lanes] - peak) * factor)
                total = total + expo[:, :128] + expo[:, 128:]
                grown = grown + dot(expo.astype(bf16), kx[tile, :, cols])
            ctx_acc[...] += grown
            return total

        total = lax.fori_loop(0, 8, one, jnp.zeros((CHUNK, 128), f32))
        total = jnp.sum(total, axis=1, keepdims=True)
        context = (ctx_acc[...] / total).astype(bf16)
        for k in range(chunk_heads):
            head = c * chunk_heads + k
            value = dot(context[k * TOK : (k + 1) * TOK], av[head])
            ho[c, x, :, k * VD : (k + 1) * VD] = value.astype(bf16)
        head_out_send(c, where["x+"], x, c * 3 + 2)
        head_out_send(c, where["x-"], x, c * 3 + 0)
        if c > 0:
            head_out_forward(c - 1)
        if c == 1:
            weight_step(3)
    head_out_forward(CHUNKS - 1)
    weight_step(4)
    for dz in range(NZ):
        for half in range(2):
            index = dz * 2 + half
            nz = lax.rem(z + dz, NZ)
            there = wf.at[
                pl.ds((1 - core) * 8 + half * 4, 4), pl.ds(pl.multiple_of(nz * 16, 16), 16), :
            ]
            remote(there, there, w3_send.at[0], w3_recv.at[index], sibling).wait_recv()

    for c in range(CHUNKS):
        head_out_wait(c, 2)
        part = dot(
            ho[c].reshape(NX * TOK, chunk_heads * VD),
            wf[c * chunk_heads : (c + 1) * chunk_heads].reshape(chunk_heads * VD, COLS),
        )
        if c == 0:
            acc[...] = part
        else:
            acc[...] += part
    outs[...] = acc[...].astype(bf16).reshape(NX, TOK, COLS)

    def result_copy(nx):
        return remote(
            outs.at[nx], rcv.at[y], out_send.at[nx], out_recv.at[y], ((z * NX + nx) * 2 + core, x)
        )

    for dx in range(NX):
        nx = lax.rem(x + dx, NX)
        if dx == 0:
            here = x == y

            @pl.when(here)
            def _():
                pltpu.make_async_copy(outs.at[nx], rcv.at[y], out_recv.at[y]).start()

            @pl.when(jnp.logical_not(here))
            def _():
                result_copy(nx).start()
        else:
            result_copy(nx).start()
    final = jnp.zeros((TOK, COLS), f32)
    for k in range(NY):
        pltpu.make_async_copy(rcv.at[k], rcv.at[k], out_recv.at[k]).wait()
        final = final + rcv[k].astype(f32)
    out_ref[...] = final.astype(bf16)

    for dx in range(NX):
        nx = lax.rem(x + dx, NX)
        if dx == 0:

            @pl.when(x != y)
            def _():
                result_copy(nx).wait_send()
        else:
            result_copy(nx).wait_send()
    for copy in pending + column_sends + weight_sends + line_sends + ring_sends + exchange:
        copy.wait_send()
    for k in range(2):
        remote(slot_ref(0), slot_ref(0), key_send.at[60 + k], key_recv.at[0], sibling).wait_send()
    for p in range(32):
        remote(slot_ref(p), slot_ref(p), sib_send.at[p], sib_recv.at[p], sibling).wait_send()


def body(
    query_plain,
    query_rotary,
    latent_cache,
    key_rotary,
    latent_gain,
    positions,
    absorb_keys,
    absorb_values,
    output_weight,
):
    f32, bf16 = jnp.float32, jnp.bfloat16
    place = positions.astype(f32)
    pos = jnp.broadcast_to(place[:, None], (TOK, 128))
    half = ROPE // 2
    frequency = rope_base ** (-jnp.arange(half, dtype=f32) / half)
    angles = place[:, None] * jnp.tile(frequency, 4)[None, :]
    sign = jnp.where((jnp.arange(128) & (ROPE - 1)) < half, -1.0, 1.0).astype(f32)
    cosine = jnp.cos(angles)
    sine = jnp.sin(angles) * sign[None, :]
    vmem = pl.BlockSpec(memory_space=pltpu.VMEM)
    hbm = pl.BlockSpec(memory_space=pl.ANY)
    dma = pltpu.SemaphoreType.DMA
    call = pl.pallas_call(
        kernel,
        out_shape=jax.ShapeDtypeStruct((TOK, COLS), bf16),
        in_specs=[vmem] * 8 + [hbm] * 2 + [vmem],
        out_specs=vmem,
        scratch_shapes=[
            pltpu.VMEM((HEADS, NOPE, LAT), bf16),
            pltpu.VMEM((HEADS, LAT, VD), bf16),
            pltpu.VMEM((8, 8 * HALF, WIDE), bf16),
            pltpu.VMEM((HEADS, TOK, NOPE), bf16),
            pltpu.VMEM((HEADS, TOK, LAT + 256), bf16),
            pltpu.VMEM((8, ROWS, 2 * CHUNK), f32),
            pltpu.VMEM((ROWS, 128), f32),
            pltpu.VMEM((8, 8, 2 * CHUNK), f32),
            pltpu.VMEM((8, 2 * CHUNK), f32),
            pltpu.VMEM((NZ, 8, 2 * CHUNK), f32),
            pltpu.VMEM((8, 8, 2 * CHUNK), f32),
            pltpu.VMEM((8, 16, COLS), bf16),
            pltpu.VMEM((HEADS, VD, COLS), bf16),
            pltpu.VMEM((CHUNK, LAT), f32),
            pltpu.VMEM((CHUNKS, NX, TOK, CHUNK // TOK * VD), bf16),
            pltpu.VMEM((NX * TOK, COLS), f32),
            pltpu.VMEM((NX, TOK, COLS), bf16),
            pltpu.VMEM((NY, TOK, COLS), bf16),
            dma((3,)),
            dma((62,)),
            dma((32,)),
            dma((32,)),
            dma((32,)),
            dma((16,)),
            dma((16,)),
            dma((8,)),
            dma((8,)),
            dma((32,)),
            dma((16,)),
            dma((16,)),
            dma((16,)),
            dma((12,)),
            dma((12,)),
            dma((4,)),
            dma((4,)),
        ],
        compiler_params=pltpu.CompilerParams(
            collective_id=0, has_side_effects=True, vmem_limit_bytes=60 * 1024 * 1024
        ),
        cost_estimate=pl.CostEstimate(
            flops=11_000_000_000, bytes_accessed=6_000_000, transcendentals=4_200_000
        ),
    )
    return call(
        query_plain.reshape(ROWS, NOPE),
        query_rotary.reshape(ROWS, ROPE),
        latent_cache,
        key_rotary,
        latent_gain.reshape(1, LAT),
        pos,
        cosine,
        sine,
        absorb_keys,
        absorb_values,
        output_weight.reshape(2 * HEADS, -1),
    )


def solution(mesh):
    return jax.shard_map(
        body,
        mesh=mesh,
        in_specs=(
            P("ctx", "head", None),
            P("ctx", "head", None),
            P("ctx", None),
            P("ctx", None),
            P(),
            P("ctx"),
            P("head", None, None),
            P("head", None, None),
            P("head", "ctx", None),
        ),
        out_specs=P("ctx", "head"),
        check_vma=False,
    )
```

time: 418 us -> 81.7 us (0.20)
  the two profiles are of different devices: /device:TPU:2 before, /device:TPU:9 now
where the time goes in v1:
time: 81.7 us; the launch traced here: 81.5 us
  Pallas kernels  76 us (93%)
  local copies, waits for them, and re-layouts  4.03 us (5%)
  other arithmetic  1.49 us (2%)
    pallas_call x1, Pallas kernels, body(): call(query_plain.reshape(ROWS, NOPE), query_rotary.reshape(ROWS, ROPE), l...  76 us
    reshape x1, local copies, waits for them, and re-layouts, body(): output_weight.reshape(2 * HEADS, -1)  1.7 us

profile of v1, /device:TPU:9, one launch (start us, length us, event | category | flops | bytes accessed | tf_op | source)
XLA Modules:
  0.0 81.5 jit_solution(8656103239666950716)
XLA Ops:
  0.0 0.7 convert_element_type.3
  0.7 0.1 mul.10
  0.8 0.7 broadcast_in_dim.16.pos_ref
  1.5 0.8 %fusion = (f32[64,128]{1,0:T(8,128)}, f32[64,128]{1,0:T(8,128)}) fusion(f32[128]{0:T(128)S(1)} %compare_select_fusion, f32[128]{0:T(128)S(1)} %mul.10, f32[64]{0:T(128)S(1)} %convert_element_type.3), kind=kLoop, calls=%fused_computation.2 | loop fusion | flops 16384 | bytes 66816 | tf_op jit(solution)/shard_map/mul | solution.py:543
  2.3 1.7 %reshape.29.w_ref = bf16[32,3584]{1,0:T(8,128)(2,1)} reshape(bf16[16,2,3584]{2,1,0:T(2,128)(2,1)} %param.17) | data formatting | bytes 458752 | tf_op jit(solution)/shard_map/reshape | solution.py:607
  4.0 76.0 %shard_map.91 = bf16[64,896]{1,0:T(8,128)(2,1)} custom-call(bf16[1024,128]{1,0:T(8,128)(2,1)} %bitcast.3, bf16[1024,64]{1,0:T(8,128)(2,1)} %bitcast.4, bf16[64,512]{1,0:T(8,128)(2,1)} %lat_ref.1, bf16[64,64]{1,0:T(8,128)(2,1)} %kr_ref.1, f32[1,512]{1,0:T(1,128)} %bitcast.5, f32[64,128]{1,0:T(8,128)} %broadcast_in_dim.16.pos_ref, ...), custom_call_target="tpu_custom_call" | custom-call | flops 11000000512 | bytes 6000000 | tf_op jit(solution)/shard_map/pallas_call | solution.py:596
  80.0 1.6 %copy.11 = bf16[64,896]{1,0:T(8,128)(2,1)} copy(bf16[64,896]{1,0:T(8,128)(2,1)} %shard_map.91) | data formatting | bytes 229376
  (3 shorter events, 0.0 us)

commit v2 on v1

v2 whole, which is shorter than its diff:
```python
import jax
import jax.numpy as jnp
import numpy as np
from jax import lax
from jax.experimental import pallas as pl
from jax.experimental.pallas import tpu as pltpu
from jax.sharding import PartitionSpec as P

MESH = pl.DeviceIdType.MESH
norm_epsilon = 1e-06
rope_base = 10000.0
masked_score = -1e30

NZ, NX, NY = 8, 4, 4
TOK = 64
HALF = 32
HEADS = 16
ROWS = TOK * HEADS
NOPE, ROPE, LAT, VD = 128, 64, 512, 128
COLS = 896
KEYS = 2 * LAT + 2 * ROPE
WIDE = KEYS + 128
SCALE = 192 ** (-0.5)
LOG2E = 1.4426950408889634

SLOTS = [
    "own", "R1", "L1", "m0", "p0", "R2", "L2", "o0",
    "Ym", "Yp", "Yo", "R3", "L3", "R4", "mR3", "pR3",
    "Amm", "Apm", "Amp", "App", "Aom", "Aop", "Amo", "Apo",
    "Aoo", "oR3", "mL3", "pL3", "oL3", "mR4", "pR4", "oR4",
]
SLOT = {name: i for i, name in enumerate(SLOTS)}


def along_x(name):
    return [("x+", "m" + name), ("x-", "p" + name), ("xx", "o" + name)]


def along_y(name):
    return [("y+", "Am" + name), ("y-", "Ap" + name), ("yy", "Ao" + name)]


FORWARD = {
    "own": [("z+", "R1"), ("z-", "L1"), ("z++", "R2"), ("z--", "L2"), ("x+", "m0"), ("x-", "p0")],
    "m0": [("x+", "o0")],
    "R2": [("z+", "R3"), ("z++", "R4")],
    "L2": [("z-", "L3")],
    "R3": along_x("R3"),
    "L3": along_x("L3"),
    "R4": along_x("R4"),
    "Ym": along_y("m"),
    "Yp": along_y("p"),
    "Yo": along_y("o"),
}
SHARED = {"R1": 0, "L1": 1, "R2": 2, "L2": 3}
SHARED_TO = (("x+", "Ym"), ("x-", "Yp"), ("xx", "Yo"))


def kernel(
    pos_ref, qp_ref, qr_ref, lat_ref, kr_ref, gain_ref, cos_g, sin_g, cos_i, sin_i, ak_hbm, av_hbm, w_ref,
    out_ref,
    ak, av, kx, qh, q2, s_buf, top, wp, wf, ho, outs, rcv,
    local_sem, key_send, key_recv, sib_send, sib_recv, w1_send, w1_recv,
    w2_send, w2_recv, w3_send, w3_recv, ho_send, ho_recv, out_send, out_recv,
):
    f32, bf16 = jnp.float32, jnp.bfloat16
    me = lax.axis_index("ctx")
    y = lax.axis_index("head")
    core = lax.rem(me, 2)
    x = lax.rem(me // 2, NX)
    z = me // (2 * NX)

    def device(dz=0, dx=0, dc=0, dy=0):
        nz = lax.rem(z + (dz + NZ), NZ)
        nx = lax.rem(x + (dx + NX), NX)
        nc = lax.rem(core + dc, 2)
        ny = lax.rem(y + (dy + NY), NY)
        return ((nz * NX + nx) * 2 + nc, ny)

    sibling = device(dc=1)
    where = {
        "z+": device(dz=1), "z-": device(dz=-1), "x+": device(dx=1), "x-": device(dx=-1),
        "y+": device(dy=1), "y-": device(dy=-1),
        "z++": device(dz=2), "z--": device(dz=-2), "xx": device(dx=2), "yy": device(dy=2),
    }
    column_peers = [device(dz=d) for d in range(1, NZ)]
    chip_peers = [(dx, dc) for dx in range(NX) for dc in range(2) if (dx, dc) != (0, 0)]
    plane_peers = [device(dx=dx, dy=dy) for dx in range(NX) for dy in range(1, NY)]
    partners = column_peers + [device(dx=a, dc=b) for a, b in chip_peers] + plane_peers

    barrier = pltpu.get_barrier_semaphore()
    for partner in partners:
        pl.semaphore_signal(barrier, inc=1, device_id=partner, device_id_type=MESH)

    load_ak = pltpu.make_async_copy(ak_hbm, ak, local_sem.at[0])
    load_av = pltpu.make_async_copy(av_hbm, av, local_sem.at[1])
    load_ak.start()
    load_av.start()

    def remote(src, dst, send, recv, to):
        return pltpu.make_async_remote_copy(
            src_ref=src, dst_ref=dst, send_sem=send, recv_sem=recv, device_id=to, device_id_type=MESH
        )

    def dot(a, b):
        return jnp.dot(a, b, preferred_element_type=f32)

    def iota(shape, axis):
        return lax.broadcasted_iota(jnp.int32, shape, axis)

    def onehot(mask):
        return jnp.where(mask, 1.0, 0.0).astype(bf16)

    def slot_ref(p, sib=0):
        return kx.at[2 * (p // 8) + sib, pl.ds((p % 8) * HALF, HALF), :]

    pending = []

    def send_block(p, to, dst):
        index = len(pending)
        copy = remote(slot_ref(p), slot_ref(dst), key_send.at[index], key_recv.at[dst], to)
        copy.start()
        pending.append(copy)

    def to_sibling(p):
        remote(slot_ref(p), slot_ref(p, 1), sib_send.at[p], sib_recv.at[p], sibling).start()

    def filled(name):
        p = SLOT[name]
        for direction, dst in FORWARD.get(name, []):
            send_block(p, where[direction], SLOT[dst])
        to_sibling(p)
        if name in SHARED:

            @pl.when(y == SHARED[name])
            def _():
                for k, (direction, dst) in enumerate(SHARED_TO):
                    remote(
                        slot_ref(p), slot_ref(SLOT[dst]), key_send.at[60 + k],
                        key_recv.at[SLOT[dst]], where[direction],
                    ).start()

    def arrived(name):
        p = SLOT[name]
        remote(slot_ref(p), slot_ref(p), key_send.at[0], key_recv.at[p], sibling).wait_recv()
        filled(name)

    raw = lat_ref[...].astype(f32)
    spread = jnp.sum(raw * raw, axis=-1, keepdims=True) * (1.0 / LAT)
    latent = (raw * lax.rsqrt(spread + norm_epsilon) * gain_ref[...]).astype(bf16)
    row_i, col_i = iota((ROPE, 128), 0), iota((ROPE, 128), 1)
    low = iota((HALF, 128), 1) < ROPE
    kr = kr_ref[...]
    first = onehot(col_i == row_i)
    second = onehot(col_i == row_i + ROPE)
    turned = (row_i + HALF) & (ROPE - 1)
    first_turned = onehot(col_i == turned)
    second_turned = onehot(col_i == turned + ROPE)
    straight = dot(kr[:HALF], first) + dot(kr[HALF:], second)
    crossed = dot(kr[:HALF], first_turned) + dot(kr[HALF:], second_turned)
    groups = [pos_ref[0] >> 5, pos_ref[HALF] >> 5]
    cosines, sines = [], []
    for g in groups:
        c_g, s_g = cos_g[pl.ds(g, 1), :], sin_g[pl.ds(g, 1), :]
        cosines.append(c_g * cos_i[...] - s_g * sin_i[...])
        sines.append(s_g * cos_i[...] + c_g * sin_i[...])
    minus = jnp.where((iota((TOK, 128), 1) & (ROPE - 1)) < HALF, -1.0, 1.0)
    cosine = jnp.concatenate(cosines, axis=0)
    sine = jnp.concatenate(sines, axis=0) * minus
    key_rot = straight * jnp.where(low, cosine[:HALF], cosine[HALF:]) + crossed * jnp.where(
        low, sine[:HALF], sine[HALF:]
    )
    lane = iota((HALF, 128), 1)
    marks = jnp.where(
        lane == 0, groups[0].astype(f32), jnp.where(lane == 1, groups[1].astype(f32), 0.0)
    )
    kx[0, 0:HALF, 0:LAT] = latent[:HALF]
    kx[0, 0:HALF, LAT : LAT + 128] = key_rot.astype(bf16)
    kx[0, 0:HALF, LAT + 128 : KEYS] = latent[HALF:]
    kx[0, 0:HALF, KEYS:WIDE] = marks.astype(bf16)

    big_i, big_j = iota((256, 256), 0), iota((256, 256), 1)
    swap = onehot(big_j == ((big_i & 15) << 4) + (big_i >> 4))
    doubled = jnp.concatenate(
        [first + second, first_turned + second_turned], axis=1
    )
    low_q = iota((256, 128), 1) < ROPE
    for b in range(TOK // 16):
        rows = slice(b * 256, (b + 1) * 256)
        plain = dot(swap, qp_ref[rows, :]).astype(bf16).reshape(HEADS, 16, NOPE)
        qh[:, b * 16 : (b + 1) * 16, :] = plain
        both = dot(swap, dot(qr_ref[rows, :], doubled).astype(bf16))
        tokens = slice(b * 16, (b + 1) * 16)
        c_rows = jnp.concatenate([cosine[tokens]] * HEADS, axis=0)
        s_rows = jnp.concatenate([sine[tokens]] * HEADS, axis=0)
        turned_q = both[:, :128] * c_rows + both[:, 128:] * s_rows
        q_first = jnp.where(low_q, turned_q, 0.0).astype(bf16).reshape(HEADS, 16, 128)
        q_second = jnp.where(low_q, 0.0, turned_q).astype(bf16).reshape(HEADS, 16, 128)
        there = slice((b % 2) * 16, (b % 2) * 16 + 16)
        q2[b // 2, :, there, 0:128] = q_second
        q2[b // 2, :, there, 128 + LAT :] = q_first
    load_ak.wait()
    for h in range(HEADS):
        absorbed = dot(qh[h], ak[h]).astype(bf16)
        q2[0, h, :, 128 : 128 + LAT] = absorbed[:HALF]
        q2[1, h, :, 128 : 128 + LAT] = absorbed[HALF:]

    pl.semaphore_wait(barrier, len(partners))

    filled("own")

    def weight_piece(nx, nc):
        return w_ref.at[
            pl.ds(pl.multiple_of(nc * 16, 16), 16), pl.ds(pl.multiple_of(nx * COLS, 128), COLS)
        ]

    my_place = x * 2 + core
    weight_sends = []
    for k, (dx, dc) in enumerate(chip_peers):
        nx, nc = lax.rem(x + dx, NX), lax.rem(core + dc, 2)
        copy = remote(
            weight_piece(nx, nc), wp.at[my_place], w1_send.at[k], w1_recv.at[my_place],
            device(dx=dx, dc=dc),
        )
        copy.start()
        weight_sends.append(copy)
    own_weight = pltpu.make_async_copy(weight_piece(x, core), wp.at[my_place], local_sem.at[2])
    own_weight.start()

    for name in SLOTS[1:14]:
        arrived(name)

    token = iota((HALF, 1), 0)
    query_pos = jnp.concatenate(
        [((g << 5) + token).astype(f32) for g in groups for h in range(HEADS)], axis=0
    )
    contract = (((1,), (1,)), ((), ()))
    inside = (iota((1, 256), 1) & (HALF - 1)).astype(f32)
    pick_i = iota((16, 128), 1)
    picks = [onehot(pick_i == part) for part in range(2)]

    def scores(tile):
        q_a = q2[:, :, :, 128:].reshape(ROWS, LAT + 128)
        q_b = q2[:, :, :, 0 : LAT + 128].reshape(ROWS, LAT + 128)
        best = None
        for part, (q, k) in enumerate(
            ((q_a, kx[tile, :, 0 : LAT + 128]), (q_b, kx[tile, :, LAT:KEYS]))
        ):
            group = lax.dot_general(
                picks[part], kx[tile, :, KEYS:WIDE], contract, preferred_element_type=f32
            )[0:1, :]
            key_pos = group * float(HALF) + inside
            s = lax.dot_general(q, k, contract, preferred_element_type=f32)
            s = jnp.where(key_pos <= query_pos, s, masked_score)
            s_buf[tile, :, part * 256 : (part + 1) * 256] = s
            high = jnp.maximum(s[:, :128], s[:, 128:])
            best = high if best is None else jnp.maximum(best, high)
        if tile == 0:
            top[...] = best
        else:
            top[...] = jnp.maximum(top[...], best)

    def from_sibling(stage):
        for p in range(stage * 8, stage * 8 + 8):
            remote(
                slot_ref(p, 1), slot_ref(p, 1), sib_send.at[p], sib_recv.at[p], sibling
            ).wait_recv()

    scores(0)

    for k, (dx, dc) in enumerate(chip_peers):
        place = lax.rem(x + dx, NX) * 2 + lax.rem(core + dc, 2)
        remote(wp.at[place], wp.at[place], w1_send.at[0], w1_recv.at[place], sibling).wait_recv()
    own_weight.wait()
    to_i, from_i = iota((128, 128), 0), iota((128, 128), 1)
    regroup = onehot(
        from_i == (((to_i & 15) >> 1) << 4) + ((to_i >> 4) << 1) + (to_i & 1)
    )
    share = dot(regroup, wp[...].reshape(128, COLS)).astype(bf16).reshape(8, 16, COLS)

    def weight_slot(dz, half):
        nz = lax.rem(z + (dz + NZ), NZ)
        return wf.at[
            pl.ds(core * 8 + half * 4, 4), pl.ds(pl.multiple_of(nz * 16, 16), 16), :
        ]

    wf[pl.ds(core * 8, 8), pl.ds(pl.multiple_of(z * 16, 16), 16), :] = share
    ring_sends = []

    def weight_on(dz, half):
        index = (dz % NZ) * 2 + half
        here = weight_slot(dz, half)
        copy = remote(here, here, w3_send.at[index], w3_recv.at[index], sibling)
        copy.start()
        ring_sends.append(copy)
        steps = []
        if -3 < dz <= 0 or (dz == -3 and half == 0):
            steps.append(("z+", dz - 1))
        if 0 <= dz < 3 or (dz == 3 and half == 1):
            steps.append(("z-", dz + 1))
        for direction, there in steps:
            arrival = (there % NZ) * 2 + half
            copy = remote(
                here, here, w2_send.at[len(ring_sends) - 1], w2_recv.at[arrival], where[direction]
            )
            copy.start()
            ring_sends.append(copy)

    def weight_arrived(dz, half):
        index = (dz % NZ) * 2 + half
        here = weight_slot(dz, half)
        remote(here, here, w2_send.at[0], w2_recv.at[index], sibling).wait_recv()
        weight_on(dz, half)

    def weight_step(step):
        for half in range(2):
            if step < 4:
                weight_arrived(-step, half)
                weight_arrived(step, half)
            else:
                weight_arrived(-4 if half == 0 else 4, half)

    weight_on(0, 0)
    weight_on(0, 1)

    from_sibling(0)
    scores(1)
    for name in SLOTS[14:24]:
        arrived(name)
    scores(2)
    from_sibling(1)
    scores(3)
    for name in SLOTS[24:29]:
        arrived(name)
    scores(4)
    from_sibling(2)
    scores(5)
    weight_step(1)
    for name in SLOTS[29:32]:
        arrived(name)
    scores(6)
    from_sibling(3)
    scores(7)
    weight_step(2)

    load_av.wait()
    factor = SCALE * LOG2E
    chunk_rows = HALF * HEADS
    exchange = []
    for c in range(2):
        rows = slice(c * chunk_rows, (c + 1) * chunk_rows)
        peak = jnp.max(top[rows, :], axis=1, keepdims=True)
        total = jnp.zeros((chunk_rows, 128), f32)
        context = jnp.zeros((chunk_rows, LAT), f32)
        for tile in range(8):
            for part, cols in enumerate((slice(0, LAT), slice(LAT + 128, KEYS))):
                expo = jnp.exp2(
                    (s_buf[tile, rows, part * 256 : (part + 1) * 256] - peak) * factor
                )
                total = total + expo[:, :128] + expo[:, 128:]
                context = context + dot(expo.astype(bf16), kx[tile, :, cols])
        context = (context / jnp.sum(total, axis=1, keepdims=True)).astype(bf16)
        for h in range(HEADS):
            value = dot(context[h * HALF : (h + 1) * HALF], av[h])
            ho[c, x, :, h * VD : (h + 1) * VD] = value.astype(bf16)
        for k, direction in enumerate(("x+", "x-", "xx")):
            piece = ho.at[c, x]
            copy = remote(
                piece, piece, ho_send.at[c * 3 + k], ho_recv.at[c * 3 + k], where[direction]
            )
            copy.start()
            exchange.append(copy)
        weight_step(3 + c)
    for dz in range(NZ):
        for half in range(2):
            index = dz * 2 + half
            nz = lax.rem(z + dz, NZ)
            there = wf.at[
                pl.ds((1 - core) * 8 + half * 4, 4), pl.ds(pl.multiple_of(nz * 16, 16), 16), :
            ]
            remote(there, there, w3_send.at[0], w3_recv.at[index], sibling).wait_recv()

    def result_copy(c, nx):
        return remote(
            outs.at[c, nx], rcv.at[c, y], out_send.at[c * NX + nx], out_recv.at[c * NY + y],
            ((z * NX + nx) * 2 + core, x),
        )

    here = x == y
    for c in range(2):
        for k, dx in enumerate((3, 1, 2)):
            piece = ho.at[c, lax.rem(x + dx, NX)]
            remote(piece, piece, ho_send.at[0], ho_recv.at[c * 3 + k], sibling).wait_recv()
        product = dot(ho[c].reshape(NX * HALF, HEADS * VD), wf[...].reshape(HEADS * VD, COLS))
        outs[c] = product.astype(bf16).reshape(NX, HALF, COLS)
        for dx in (2, 1, 3, 0):
            nx = lax.rem(x + dx, NX)
            if dx == 0:

                @pl.when(here)
                def _():
                    pltpu.make_async_copy(
                        outs.at[c, nx], rcv.at[c, y], out_recv.at[c * NY + y]
                    ).start()

                @pl.when(jnp.logical_not(here))
                def _():
                    result_copy(c, nx).start()
            else:
                result_copy(c, nx).start()
    for c in range(2):
        final = jnp.zeros((HALF, COLS), f32)
        for k in range(NY):
            pltpu.make_async_copy(rcv.at[c, k], rcv.at[c, k], out_recv.at[c * NY + k]).wait()
            final = final + rcv[c, k].astype(f32)
        out_ref[c * HALF : (c + 1) * HALF, :] = final.astype(bf16)

    for c in range(2):
        for dx in range(NX):
            nx = lax.rem(x + dx, NX)
            if dx == 0:

                @pl.when(jnp.logical_not(here))
                def _():
                    result_copy(c, nx).wait_send()
            else:
                result_copy(c, nx).wait_send()
    for copy in pending + weight_sends + ring_sends + exchange:
        copy.wait_send()
    for k in range(len(SHARED_TO)):
        remote(slot_ref(0), slot_ref(0), key_send.at[60 + k], key_recv.at[0], sibling).wait_send()
    for p in range(32):
        remote(slot_ref(p), slot_ref(p), sib_send.at[p], sib_recv.at[p], sibling).wait_send()


def body(
    query_plain,
    query_rotary,
    latent_cache,
    key_rotary,
    latent_gain,
    positions,
    absorb_keys,
    absorb_values,
    output_weight,
):
    f32, bf16 = jnp.float32, jnp.bfloat16
    frequency = np.tile(rope_base ** (-np.arange(ROPE // 2) / (ROPE // 2)), 4)[None, :]
    inner = np.arange(HALF)[:, None] * frequency
    outer = np.arange(0, 4096, HALF)[:, None] * frequency
    tables = [f(a).astype(np.float32) for a in (outer, inner) for f in (np.cos, np.sin)]
    vmem = pl.BlockSpec(memory_space=pltpu.VMEM)
    hbm = pl.BlockSpec(memory_space=pl.ANY)
    dma = pltpu.SemaphoreType.DMA
    call = pl.pallas_call(
        kernel,
        out_shape=jax.ShapeDtypeStruct((TOK, COLS), bf16),
        in_specs=[pl.BlockSpec(memory_space=pltpu.SMEM)] + [vmem] * 9 + [hbm] * 2 + [vmem],
        out_specs=vmem,
        scratch_shapes=[
            pltpu.VMEM((HEADS, NOPE, LAT), bf16),
            pltpu.VMEM((HEADS, LAT, VD), bf16),
            pltpu.VMEM((8, 8 * HALF, WIDE), bf16),
            pltpu.VMEM((HEADS, TOK, NOPE), bf16),
            pltpu.VMEM((2, HEADS, HALF, LAT + 256), bf16),
            pltpu.VMEM((8, ROWS, 512), f32),
            pltpu.VMEM((ROWS, 128), f32),
            pltpu.VMEM((8, 16, COLS), bf16),
            pltpu.VMEM((HEADS, VD, COLS), bf16),
            pltpu.VMEM((2, NX, HALF, HEADS * VD), bf16),
            pltpu.VMEM((2, NX, HALF, COLS), bf16),
            pltpu.VMEM((2, NY, HALF, COLS), bf16),
            dma((3,)),
            dma((63,)),
            dma((32,)),
            dma((32,)),
            dma((32,)),
            dma((8,)),
            dma((8,)),
            dma((32,)),
            dma((16,)),
            dma((16,)),
            dma((16,)),
            dma((6,)),
            dma((6,)),
            dma((8,)),
            dma((8,)),
        ],
        compiler_params=pltpu.CompilerParams(
            collective_id=0, has_side_effects=True, vmem_limit_bytes=60 * 1024 * 1024
        ),
        cost_estimate=pl.CostEstimate(
            flops=11_000_000_000, bytes_accessed=6_000_000, transcendentals=4_200_000
        ),
    )
    return call(
        positions,
        query_plain.reshape(ROWS, NOPE),
        query_rotary.reshape(ROWS, ROPE),
        latent_cache,
        key_rotary,
        latent_gain.reshape(1, LAT),
        *tables,
        absorb_keys,
        absorb_values,
        output_weight.reshape(2 * HEADS, -1),
    )


def solution(mesh):
    return jax.shard_map(
        body,
        mesh=mesh,
        in_specs=(
            P("ctx", "head", None),
            P("ctx", "head", None),
            P("ctx", None),
            P("ctx", None),
            P(),
            P("ctx"),
            P("head", None, None),
            P("head", None, None),
            P("head", "ctx", None),
        ),
        out_specs=P("ctx", "head"),
        check_vma=False,
    )
```

time: 81.7 us -> 73 us (0.89)
  the two profiles are of different devices: /device:TPU:9 before, /device:TPU:2 now
where the time goes in v2:
time: 73 us; the launch traced here: 72.9 us
  Pallas kernels  69.6 us (95%)
  local copies, waits for them, and re-layouts  3.25 us (4%)
    pallas_call x1, Pallas kernels, body(): call(positions, query_plain.reshape(ROWS, NOPE), query_rotary.reshape(ROW...  69.6 us
    reshape x1, local copies, waits for them, and re-layouts, body(): output_weight.reshape(2 * HEADS, -1)  1.7 us
    unnamed x1, local copies, waits for them, and re-layouts  1.55 us

profile of v2, /device:TPU:2, one launch (start us, length us, event | category | flops | bytes accessed | tf_op | source)
XLA Modules:
  0.0 72.9 jit_solution(14532308083567244951)
XLA Ops:
  0.0 1.7 %reshape.15.w_ref = bf16[32,3584]{1,0:T(8,128)(2,1)} reshape(bf16[16,2,3584]{2,1,0:T(2,128)(2,1)} %param.21) | data formatting | bytes 458752 | tf_op jit(solution)/shard_map/reshape | solution.py:506
  1.7 69.6 %shard_map.127 = bf16[64,896]{1,0:T(8,128)(2,1)} custom-call(s32[64]{0:T(128)} %pos_ref.1, bf16[1024,128]{1,0:T(8,128)(2,1)} %bitcast.3, bf16[1024,64]{1,0:T(8,128)(2,1)} %bitcast.4, bf16[64,512]{1,0:T(8,128)(2,1)} %lat_ref.1, bf16[64,64]{1,0:T(8,128)(2,1)} %kr_ref.1, f32[1,512]{1,0:T(1,128)} %bitcast.5, f32[128,128]{1,0:T(8,128)} %constant.8.clone.cos_g, ...), custom_call_target="tpu_custom_call" | custom-call | flops 11000000512 | bytes 6000000 | tf_op jit(solution)/shard_map/pallas_call | solution.py:496
  71.3 1.6 %copy.15 = bf16[64,896]{1,0:T(8,128)(2,1)} copy(bf16[64,896]{1,0:T(8,128)(2,1)} %shard_map.127) | data formatting | bytes 229376

commit v3 on v2

--- a/solution.py
+++ b/solution.py
@@ -14,6 +14,8 @@
 NZ, NX, NY = 8, 4, 4
 TOK = 64
 HALF = 32
+PART = 16
+CHUNKS = TOK // PART
 HEADS = 16
 ROWS = TOK * HEADS
 NOPE, ROPE, LAT, VD = 128, 64, 512, 128
@@ -57,9 +59,11 @@
 
 
 def kernel(
-    pos_ref, qp_ref, qr_ref, lat_ref, kr_ref, gain_ref, cos_g, sin_g, cos_i, sin_i, ak_hbm, av_hbm, w_ref,
+    pos_hbm, qp_hbm, qr_hbm, lat_hbm, kr_hbm, gain_hbm, cos_g_hbm, sin_g_hbm, cos_i_hbm, sin_i_hbm, ak_hbm, av_hbm,
+    w_hbm,
     out_ref,
-    ak, av, kx, qh, q2, s_buf, top, wp, wf, ho, outs, rcv,
+    pos_ref, qp_ref, qr_ref, lat_ref, kr_ref, gain_ref, cos_g, sin_g, cos_i, sin_i,
+    ak, av, kx, qh, q2, s_buf, top, running_top, running_total, context_sum, wp, wf, ho, outs, rcv,
     local_sem, key_send, key_recv, sib_send, sib_recv, w1_send, w1_recv,
     w2_send, w2_recv, w3_send, w3_recv, ho_send, ho_recv, out_send, out_recv,
 ):
@@ -94,6 +98,18 @@
 
     load_ak = pltpu.make_async_copy(ak_hbm, ak, local_sem.at[0])
     load_av = pltpu.make_async_copy(av_hbm, av, local_sem.at[1])
+    loads = [
+        pltpu.make_async_copy(source, target, local_sem.at[3 + k])
+        for k, (source, target) in enumerate(
+            (
+                (pos_hbm, pos_ref), (lat_hbm, lat_ref), (kr_hbm, kr_ref), (gain_hbm, gain_ref),
+                (cos_g_hbm, cos_g), (sin_g_hbm, sin_g), (cos_i_hbm, cos_i), (sin_i_hbm, sin_i),
+                (qp_hbm, qp_ref), (qr_hbm, qr_ref),
+            )
+        )
+    ]
+    for load in loads:
+        load.start()
     load_ak.start()
     load_av.start()
 
@@ -145,6 +161,8 @@
         remote(slot_ref(p), slot_ref(p), key_send.at[0], key_recv.at[p], sibling).wait_recv()
         filled(name)
 
+    for load in loads[:8]:
+        load.wait()
     raw = lat_ref[...].astype(f32)
     spread = jnp.sum(raw * raw, axis=-1, keepdims=True) * (1.0 / LAT)
     latent = (raw * lax.rsqrt(spread + norm_epsilon) * gain_ref[...]).astype(bf16)
@@ -185,6 +203,8 @@
         [first + second, first_turned + second_turned], axis=1
     )
     low_q = iota((256, 128), 1) < ROPE
+    for load in loads[8:]:
+        load.wait()
     for b in range(TOK // 16):
         rows = slice(b * 256, (b + 1) * 256)
         plain = dot(swap, qp_ref[rows, :]).astype(bf16).reshape(HEADS, 16, NOPE)
@@ -196,23 +216,20 @@
         turned_q = both[:, :128] * c_rows + both[:, 128:] * s_rows
         q_first = jnp.where(low_q, turned_q, 0.0).astype(bf16).reshape(HEADS, 16, 128)
         q_second = jnp.where(low_q, 0.0, turned_q).astype(bf16).reshape(HEADS, 16, 128)
-        there = slice((b % 2) * 16, (b % 2) * 16 + 16)
-        q2[b // 2, :, there, 0:128] = q_second
-        q2[b // 2, :, there, 128 + LAT :] = q_first
+        q2[b, :, :, 0:128] = q_second
+        q2[b, :, :, 128 + LAT :] = q_first
     load_ak.wait()
     for h in range(HEADS):
         absorbed = dot(qh[h], ak[h]).astype(bf16)
-        q2[0, h, :, 128 : 128 + LAT] = absorbed[:HALF]
-        q2[1, h, :, 128 : 128 + LAT] = absorbed[HALF:]
+        for b in range(CHUNKS):
+            q2[b, h, :, 128 : 128 + LAT] = absorbed[b * PART : (b + 1) * PART]
 
     pl.semaphore_wait(barrier, len(partners))
 
     filled("own")
 
     def weight_piece(nx, nc):
-        return w_ref.at[
-            pl.ds(pl.multiple_of(nc * 16, 16), 16), pl.ds(pl.multiple_of(nx * COLS, 128), COLS)
-        ]
+        return w_hbm.at[pl.ds(nc * 8, 8), :, pl.ds(pl.multiple_of(nx * COLS, 128), COLS)]
 
     my_place = x * 2 + core
     weight_sends = []
@@ -227,21 +244,24 @@
     own_weight = pltpu.make_async_copy(weight_piece(x, core), wp.at[my_place], local_sem.at[2])
     own_weight.start()
 
-    for name in SLOTS[1:14]:
-        arrived(name)
-
-    token = iota((HALF, 1), 0)
-    query_pos = jnp.concatenate(
-        [((g << 5) + token).astype(f32) for g in groups for h in range(HEADS)], axis=0
-    )
+    token = iota((PART, 1), 0)
+    query_pos = [
+        jnp.concatenate([((g << 5) + (token + start)).astype(f32)] * HEADS, axis=0)
+        for g in groups
+        for start in range(0, HALF, PART)
+    ]
     contract = (((1,), (1,)), ((), ()))
     inside = (iota((1, 256), 1) & (HALF - 1)).astype(f32)
     pick_i = iota((16, 128), 1)
     picks = [onehot(pick_i == part) for part in range(2)]
 
-    def scores(tile):
-        q_a = q2[:, :, :, 128:].reshape(ROWS, LAT + 128)
-        q_b = q2[:, :, :, 0 : LAT + 128].reshape(ROWS, LAT + 128)
+    factor = SCALE * LOG2E
+    chunk_rows = PART * HEADS
+
+    def scores(tile, c):
+        rows = slice(c * chunk_rows, (c + 1) * chunk_rows)
+        q_a = q2[c, :, :, 128:].reshape(chunk_rows, LAT + 128)
+        q_b = q2[c, :, :, 0 : LAT + 128].reshape(chunk_rows, LAT + 128)
         best = None
         for part, (q, k) in enumerate(
             ((q_a, kx[tile, :, 0 : LAT + 128]), (q_b, kx[tile, :, LAT:KEYS]))
@@ -251,14 +271,45 @@
             )[0:1, :]
             key_pos = group * float(HALF) + inside
             s = lax.dot_general(q, k, contract, preferred_element_type=f32)
-            s = jnp.where(key_pos <= query_pos, s, masked_score)
-            s_buf[tile, :, part * 256 : (part + 1) * 256] = s
+            s = jnp.where(key_pos <= query_pos[c], s, masked_score)
+            s_buf[tile % 2, rows, part * 256 : (part + 1) * 256] = s
             high = jnp.maximum(s[:, :128], s[:, 128:])
             best = high if best is None else jnp.maximum(best, high)
-        if tile == 0:
-            top[...] = best
+        top[tile % 2, rows, :] = best
+
+    def update(stage, c):
+        rows = slice(c * chunk_rows, (c + 1) * chunk_rows)
+        peak = jnp.max(jnp.maximum(top[0, rows, :], top[1, rows, :]), axis=1, keepdims=True)
+        if stage > 0:
+            before = running_top[rows, 0:1]
+            peak = jnp.maximum(before, peak)
+            shrink = jnp.exp2((before - peak) * factor)
+            total = running_total[rows, :] * shrink
         else:
-            top[...] = jnp.maximum(top[...], best)
+            total = jnp.zeros((chunk_rows, 128), f32)
+        grown = None
+        for dc in range(2):
+            tile = 2 * stage + dc
+            for part, cols in enumerate((slice(0, LAT), slice(LAT + 128, KEYS))):
+                expo = jnp.exp2((s_buf[dc, rows, part * 256 : (part + 1) * 256] - peak) * factor)
+                total = total + expo[:, :128] + expo[:, 128:]
+                product = dot(expo.astype(bf16), kx[tile, :, cols])
+                grown = product if grown is None else grown + product
+        if stage > 0:
+            grown = grown + context_sum[rows, :] * shrink
+        if stage < 3:
+            running_top[rows, :] = jnp.broadcast_to(peak, (chunk_rows, 128))
+            running_total[rows, :] = total
+            context_sum[rows, :] = grown
+        return grown, total
+
+    def scores_all(tile):
+        for c in range(CHUNKS):
+            scores(tile, c)
+
+    def update_all(stage):
+        for c in range(CHUNKS):
+            update(stage, c)
 
     def from_sibling(stage):
         for p in range(stage * 8, stage * 8 + 8):
@@ -266,25 +317,12 @@
                 slot_ref(p, 1), slot_ref(p, 1), sib_send.at[p], sib_recv.at[p], sibling
             ).wait_recv()
 
-    scores(0)
-
-    for k, (dx, dc) in enumerate(chip_peers):
-        place = lax.rem(x + dx, NX) * 2 + lax.rem(core + dc, 2)
-        remote(wp.at[place], wp.at[place], w1_send.at[0], w1_recv.at[place], sibling).wait_recv()
-    own_weight.wait()
-    to_i, from_i = iota((128, 128), 0), iota((128, 128), 1)
-    regroup = onehot(
-        from_i == (((to_i & 15) >> 1) << 4) + ((to_i >> 4) << 1) + (to_i & 1)
-    )
-    share = dot(regroup, wp[...].reshape(128, COLS)).astype(bf16).reshape(8, 16, COLS)
-
     def weight_slot(dz, half):
         nz = lax.rem(z + (dz + NZ), NZ)
         return wf.at[
             pl.ds(core * 8 + half * 4, 4), pl.ds(pl.multiple_of(nz * 16, 16), 16), :
         ]
 
-    wf[pl.ds(core * 8, 8), pl.ds(pl.multiple_of(z * 16, 16), 16), :] = share
     ring_sends = []
 
     def weight_on(dz, half):
@@ -320,57 +358,82 @@
             else:
                 weight_arrived(-4 if half == 0 else 4, half)
 
+    def events(names):
+        for name in names:
+            arrived(name)
+
+    events(SLOTS[1:8])
+    scores_all(0)
+    events(SLOTS[8:11])
+
+    for k, (dx, dc) in enumerate(chip_peers):
+        place = lax.rem(x + dx, NX) * 2 + lax.rem(core + dc, 2)
+        remote(wp.at[place], wp.at[place], w1_send.at[0], w1_recv.at[place], sibling).wait_recv()
+    own_weight.wait()
+    to_i, from_i = iota((128, 128), 0), iota((128, 128), 1)
+    regroup = onehot(
+        from_i == (((to_i & 15) >> 1) << 4) + ((to_i >> 4) << 1) + (to_i & 1)
+    )
+    share = dot(regroup, wp[...].reshape(128, COLS)).astype(bf16).reshape(8, 16, COLS)
+
+    wf[pl.ds(core * 8, 8), pl.ds(pl.multiple_of(z * 16, 16), 16), :] = share
+    from_sibling(0)
+    scores_all(1)
+    events(SLOTS[11:13])
     weight_on(0, 0)
     weight_on(0, 1)
-
-    from_sibling(0)
-    scores(1)
-    for name in SLOTS[14:24]:
-        arrived(name)
-    scores(2)
+    update_all(0)
+    events(SLOTS[13:16])
+    weight_step(1)
+    scores_all(2)
+    events(SLOTS[16:24])
     from_sibling(1)
-    scores(3)
-    for name in SLOTS[24:29]:
-        arrived(name)
-    scores(4)
+    scores_all(3)
+    update_all(1)
+    events(SLOTS[24:27])
+    weight_step(2)
+    scores_all(4)
     from_sibling(2)
-    scores(5)
-    weight_step(1)
-    for name in SLOTS[29:32]:
-        arrived(name)
-    scores(6)
+    scores_all(5)
+    update_all(2)
+    events(SLOTS[27:32])
+    scores_all(6)
+    load_av.wait()
     from_sibling(3)
-    scores(7)
-    weight_step(2)
-
-    load_av.wait()
-    factor = SCALE * LOG2E
-    chunk_rows = HALF * HEADS
+
     exchange = []
-    for c in range(2):
-        rows = slice(c * chunk_rows, (c + 1) * chunk_rows)
-        peak = jnp.max(top[rows, :], axis=1, keepdims=True)
-        total = jnp.zeros((chunk_rows, 128), f32)
-        context = jnp.zeros((chunk_rows, LAT), f32)
-        for tile in range(8):
-            for part, cols in enumerate((slice(0, LAT), slice(LAT + 128, KEYS))):
-                expo = jnp.exp2(
-                    (s_buf[tile, rows, part * 256 : (part + 1) * 256] - peak) * factor
-                )
-                total = total + expo[:, :128] + expo[:, 128:]
-                context = context + dot(expo.astype(bf16), kx[tile, :, cols])
+
+    def head_out_copy(c, k, place, direction):
+        piece = ho.at[c, place]
+        if k >= 2:
+            piece = ho.at[c, place, :, pl.ds((k - 2) * 1024, 1024)]
+        return remote(
+            piece, piece, ho_send.at[c * 4 + k], ho_recv.at[c * 4 + k], where[direction]
+        )
+
+    def head_out_send(*what):
+        copy = head_out_copy(*what)
+        copy.start()
+        exchange.append(copy)
+
+    from_left, from_right = lax.rem(x + 3, NX), lax.rem(x + 1, NX)
+    opposite = lax.rem(x + 2, NX)
+    for c in range(CHUNKS):
+        scores(7, c)
+        context, total = update(3, c)
         context = (context / jnp.sum(total, axis=1, keepdims=True)).astype(bf16)
         for h in range(HEADS):
-            value = dot(context[h * HALF : (h + 1) * HALF], av[h])
+            value = dot(context[h * PART : (h + 1) * PART], av[h])
             ho[c, x, :, h * VD : (h + 1) * VD] = value.astype(bf16)
-        for k, direction in enumerate(("x+", "x-", "xx")):
-            piece = ho.at[c, x]
-            copy = remote(
-                piece, piece, ho_send.at[c * 3 + k], ho_recv.at[c * 3 + k], where[direction]
-            )
-            copy.start()
-            exchange.append(copy)
-        weight_step(3 + c)
+        head_out_send(c, 0, x, "x+")
+        head_out_send(c, 1, x, "x-")
+    weight_step(3)
+    for c in range(CHUNKS):
+        head_out_copy(c, 0, from_left, "x+").wait_recv()
+        head_out_send(c, 2, from_left, "x+")
+        head_out_copy(c, 1, from_right, "x-").wait_recv()
+        head_out_send(c, 3, from_right, "x-")
+    weight_step(4)
     for dz in range(NZ):
         for half in range(2):
             index = dz * 2 + half
@@ -387,12 +450,11 @@
         )
 
     here = x == y
-    for c in range(2):
-        for k, dx in enumerate((3, 1, 2)):
-            piece = ho.at[c, lax.rem(x + dx, NX)]
-            remote(piece, piece, ho_send.at[0], ho_recv.at[c * 3 + k], sibling).wait_recv()
-        product = dot(ho[c].reshape(NX * HALF, HEADS * VD), wf[...].reshape(HEADS * VD, COLS))
-        outs[c] = product.astype(bf16).reshape(NX, HALF, COLS)
+    for c in range(CHUNKS):
+        head_out_copy(c, 2, opposite, "x+").wait_recv()
+        head_out_copy(c, 3, opposite, "x-").wait_recv()
+        product = dot(ho[c].reshape(NX * PART, HEADS * VD), wf[...].reshape(HEADS * VD, COLS))
+        outs[c] = product.astype(bf16).reshape(NX, PART, COLS)
         for dx in (2, 1, 3, 0):
             nx = lax.rem(x + dx, NX)
             if dx == 0:
@@ -408,14 +470,14 @@
                     result_copy(c, nx).start()
             else:
                 result_copy(c, nx).start()
-    for c in range(2):
-        final = jnp.zeros((HALF, COLS), f32)
+    for c in range(CHUNKS):
+        final = jnp.zeros((PART, COLS), f32)
         for k in range(NY):
             pltpu.make_async_copy(rcv.at[c, k], rcv.at[c, k], out_recv.at[c * NY + k]).wait()
             final = final + rcv[c, k].astype(f32)
-        out_ref[c * HALF : (c + 1) * HALF, :] = final.astype(bf16)
-
-    for c in range(2):
+        out_ref[c * PART : (c + 1) * PART, :] = final.astype(bf16)
+
+    for c in range(CHUNKS):
         for dx in range(NX):
             nx = lax.rem(x + dx, NX)
             if dx == 0:
@@ -455,22 +517,35 @@
     call = pl.pallas_call(
         kernel,
         out_shape=jax.ShapeDtypeStruct((TOK, COLS), bf16),
-        in_specs=[pl.BlockSpec(memory_space=pltpu.SMEM)] + [vmem] * 9 + [hbm] * 2 + [vmem],
+        in_specs=[hbm] * 13,
         out_specs=vmem,
         scratch_shapes=[
+            pltpu.SMEM((TOK,), jnp.int32),
+            pltpu.VMEM((ROWS, NOPE), bf16),
+            pltpu.VMEM((ROWS, ROPE), bf16),
+            pltpu.VMEM((TOK, LAT), bf16),
+            pltpu.VMEM((TOK, ROPE), bf16),
+            pltpu.VMEM((1, LAT), f32),
+            pltpu.VMEM((128, 128), f32),
+            pltpu.VMEM((128, 128), f32),
+            pltpu.VMEM((HALF, 128), f32),
+            pltpu.VMEM((HALF, 128), f32),
             pltpu.VMEM((HEADS, NOPE, LAT), bf16),
             pltpu.VMEM((HEADS, LAT, VD), bf16),
             pltpu.VMEM((8, 8 * HALF, WIDE), bf16),
             pltpu.VMEM((HEADS, TOK, NOPE), bf16),
-            pltpu.VMEM((2, HEADS, HALF, LAT + 256), bf16),
-            pltpu.VMEM((8, ROWS, 512), f32),
+            pltpu.VMEM((CHUNKS, HEADS, PART, LAT + 256), bf16),
+            pltpu.VMEM((2, ROWS, 512), f32),
+            pltpu.VMEM((2, ROWS, 128), f32),
             pltpu.VMEM((ROWS, 128), f32),
-            pltpu.VMEM((8, 16, COLS), bf16),
+            pltpu.VMEM((ROWS, 128), f32),
+            pltpu.VMEM((ROWS, LAT), f32),
+            pltpu.VMEM((8, 8, 2, COLS), bf16),
             pltpu.VMEM((HEADS, VD, COLS), bf16),
-            pltpu.VMEM((2, NX, HALF, HEADS * VD), bf16),
-            pltpu.VMEM((2, NX, HALF, COLS), bf16),
-            pltpu.VMEM((2, NY, HALF, COLS), bf16),
-            dma((3,)),
+            pltpu.VMEM((CHUNKS, NX, PART, HEADS * VD), bf16),
+            pltpu.VMEM((CHUNKS, NX, PART, COLS), bf16),
+            pltpu.VMEM((CHUNKS, NY, PART, COLS), bf16),
+            dma((13,)),
             dma((63,)),
             dma((32,)),
             dma((32,)),
@@ -481,10 +556,10 @@
             dma((16,)),
             dma((16,)),
             dma((16,)),
-            dma((6,)),
-            dma((6,)),
-            dma((8,)),
-            dma((8,)),
+            dma((4 * CHUNKS,)),
+            dma((4 * CHUNKS,)),
+            dma((NX * CHUNKS,)),
+            dma((NY * CHUNKS,)),
         ],
         compiler_params=pltpu.CompilerParams(
             collective_id=0, has_side_effects=True, vmem_limit_bytes=60 * 1024 * 1024
@@ -503,7 +578,7 @@
         *tables,
         absorb_keys,
         absorb_values,
-        output_weight.reshape(2 * HEADS, -1),
+        output_weight,
     )
 
 

time: 73 us -> 69 us (0.945)
  Pallas kernels: 69.6 us -> 66.9 us
  local copies, waits for them, and re-layouts: 3.25 us -> 1.55 us
    pallas_call x1, Pallas kernels: 69.6 us -> 66.9 us  [body(): call(positions, query_plain.reshape(ROWS, NOPE), query_rotary.reshape(ROW...]
    reshape x1 -> x0, local copies, waits for them, and re-layouts: 1.7 us -> none  [body(): output_weight.reshape(2 * HEADS, -1)]
where the time goes in v3:
time: 69 us; the launch traced here: 68.4 us
  Pallas kernels  66.9 us (97%)
  local copies, waits for them, and re-layouts  1.55 us (2%)
    pallas_call x1, Pallas kernels, body(): call(positions, query_plain.reshape(ROWS, NOPE), query_rotary.reshape(ROW...  66.9 us
    unnamed x1, local copies, waits for them, and re-layouts  1.55 us

profile of v3, /device:TPU:2, one launch (start us, length us, event | category | flops | bytes accessed | tf_op | source)
XLA Modules:
  0.0 68.4 jit_solution(9487766598655381547)
XLA Ops:
  0.0 66.9 %shard_map.127 = bf16[64,896]{1,0:T(8,128)(2,1)} custom-call(s32[64]{0:T(128)} %pos_hbm.1, bf16[1024,128]{1,0:T(8,128)(2,1)} %bitcast.3, bf16[1024,64]{1,0:T(8,128)(2,1)} %bitcast.4, bf16[64,512]{1,0:T(8,128)(2,1)} %lat_hbm.1, bf16[64,64]{1,0:T(8,128)(2,1)} %kr_hbm.1, f32[1,512]{1,0:T(1,128)} %bitcast.5, f32[128,128]{1,0:T(8,128)} %constant.8.clone.cos_g_hbm, ...), custom_call_target="tpu_custom_call" | custom-call | flops 11000000512 | bytes 6000000 | tf_op jit(solution)/shard_map/pallas_call | solution.py:571
  66.9 1.6 %copy.15 = bf16[64,896]{1,0:T(8,128)(2,1)} copy(bf16[64,896]{1,0:T(8,128)(2,1)} %shard_map.127) | data formatting | bytes 229376

commit v4 on v3

--- a/solution.py
+++ b/solution.py
@@ -332,10 +332,14 @@
         copy.start()
         ring_sends.append(copy)
         steps = []
-        if -3 < dz <= 0 or (dz == -3 and half == 0):
+        if -3 < dz <= 0:
             steps.append(("z+", dz - 1))
-        if 0 <= dz < 3 or (dz == 3 and half == 1):
+        if 0 <= dz < 3:
             steps.append(("z-", dz + 1))
+        if dz == -2 and half == 0:
+            steps.append(("z++", dz - 2))
+        if dz == 2 and half == 1:
+            steps.append(("z--", dz + 2))
         for direction, there in steps:
             arrival = (there % NZ) * 2 + half
             copy = remote(
@@ -364,7 +368,6 @@
 
     events(SLOTS[1:8])
     scores_all(0)
-    events(SLOTS[8:11])
 
     for k, (dx, dc) in enumerate(chip_peers):
         place = lax.rem(x + dx, NX) * 2 + lax.rem(core + dc, 2)
@@ -379,24 +382,27 @@
     wf[pl.ds(core * 8, 8), pl.ds(pl.multiple_of(z * 16, 16), 16), :] = share
     from_sibling(0)
     scores_all(1)
-    events(SLOTS[11:13])
+    events(["R3", "L3"])
     weight_on(0, 0)
     weight_on(0, 1)
+    events(["Ym", "Yp", "Yo"])
     update_all(0)
-    events(SLOTS[13:16])
+    events(["R4", "mR3", "pR3"])
+    scores_all(2)
     weight_step(1)
-    scores_all(2)
-    events(SLOTS[16:24])
+    events(SLOTS[16:20])
     from_sibling(1)
     scores_all(3)
+    events(SLOTS[20:24])
     update_all(1)
-    events(SLOTS[24:27])
     weight_step(2)
     scores_all(4)
     from_sibling(2)
+    events(SLOTS[24:27])
     scores_all(5)
+    events(SLOTS[27:29])
     update_all(2)
-    events(SLOTS[27:32])
+    events(SLOTS[29:32])
     scores_all(6)
     load_av.wait()
     from_sibling(3)
@@ -427,12 +433,12 @@
             ho[c, x, :, h * VD : (h + 1) * VD] = value.astype(bf16)
         head_out_send(c, 0, x, "x+")
         head_out_send(c, 1, x, "x-")
-    weight_step(3)
     for c in range(CHUNKS):
         head_out_copy(c, 0, from_left, "x+").wait_recv()
         head_out_send(c, 2, from_left, "x+")
         head_out_copy(c, 1, from_right, "x-").wait_recv()
         head_out_send(c, 3, from_right, "x-")
+    weight_step(3)
     weight_step(4)
     for dz in range(NZ):
         for half in range(2):

time: 69 us -> 68.1 us (0.987)
  Pallas kernels: 66.9 us -> 65.6 us
    pallas_call x1, Pallas kernels: 66.9 us -> 65.6 us  [body(): call(positions, query_plain.reshape(ROWS, NOPE), query_rotary.reshape(ROW...]
where the time goes in v4:
time: 68.1 us; the launch traced here: 67.2 us
  Pallas kernels  65.6 us (96%)
  local copies, waits for them, and re-layouts  1.55 us (2%)
    pallas_call x1, Pallas kernels, body(): call(positions, query_plain.reshape(ROWS, NOPE), query_rotary.reshape(ROW...  65.6 us
    unnamed x1, local copies, waits for them, and re-layouts  1.55 us

profile of v4, /device:TPU:2, one launch (start us, length us, event | category | flops | bytes accessed | tf_op | source)
XLA Modules:
  0.0 67.2 jit_solution(6418496889179453168)
XLA Ops:
  0.0 65.6 %shard_map.127 = bf16[64,896]{1,0:T(8,128)(2,1)} custom-call(s32[64]{0:T(128)} %pos_hbm.1, bf16[1024,128]{1,0:T(8,128)(2,1)} %bitcast.3, bf16[1024,64]{1,0:T(8,128)(2,1)} %bitcast.4, bf16[64,512]{1,0:T(8,128)(2,1)} %lat_hbm.1, bf16[64,64]{1,0:T(8,128)(2,1)} %kr_hbm.1, f32[1,512]{1,0:T(1,128)} %bitcast.5, f32[128,128]{1,0:T(8,128)} %constant.8.clone.cos_g_hbm, ...), custom_call_target="tpu_custom_call" | custom-call | flops 11000000512 | bytes 6000000 | tf_op jit(solution)/shard_map/pallas_call | solution.py:577
  65.6 1.6 %copy.15 = bf16[64,896]{1,0:T(8,128)(2,1)} copy(bf16[64,896]{1,0:T(8,128)(2,1)} %shard_map.127) | data formatting | bytes 229376

commit v5 on v4

--- a/solution.py
+++ b/solution.py
@@ -433,13 +433,14 @@
             ho[c, x, :, h * VD : (h + 1) * VD] = value.astype(bf16)
         head_out_send(c, 0, x, "x+")
         head_out_send(c, 1, x, "x-")
+    weight_step(3)
     for c in range(CHUNKS):
+        if c == 2:
+            weight_step(4)
         head_out_copy(c, 0, from_left, "x+").wait_recv()
         head_out_send(c, 2, from_left, "x+")
         head_out_copy(c, 1, from_right, "x-").wait_recv()
         head_out_send(c, 3, from_right, "x-")
-    weight_step(3)
-    weight_step(4)
     for dz in range(NZ):
         for half in range(2):
             index = dz * 2 + half

time: 68.1 us -> 66.7 us (0.979)
  Pallas kernels: 65.6 us -> 64.9 us
    pallas_call x1, Pallas kernels: 65.6 us -> 64.9 us  [body(): call(positions, query_plain.reshape(ROWS, NOPE), query_rotary.reshape(ROW...]
where the time goes in v5:
time: 66.7 us; the launch traced here: 66.4 us
  Pallas kernels  64.9 us (97%)
  local copies, waits for them, and re-layouts  1.55 us (2%)
    pallas_call x1, Pallas kernels, body(): call(positions, query_plain.reshape(ROWS, NOPE), query_rotary.reshape(ROW...  64.9 us
    unnamed x1, local copies, waits for them, and re-layouts  1.55 us

profile of v5, /device:TPU:2, one launch (start us, length us, event | category | flops | bytes accessed | tf_op | source)
XLA Modules:
  0.0 66.4 jit_solution(1271003289253281110)
XLA Ops:
  0.0 64.9 %shard_map.127 = bf16[64,896]{1,0:T(8,128)(2,1)} custom-call(s32[64]{0:T(128)} %pos_hbm.1, bf16[1024,128]{1,0:T(8,128)(2,1)} %bitcast.3, bf16[1024,64]{1,0:T(8,128)(2,1)} %bitcast.4, bf16[64,512]{1,0:T(8,128)(2,1)} %lat_hbm.1, bf16[64,64]{1,0:T(8,128)(2,1)} %kr_hbm.1, f32[1,512]{1,0:T(1,128)} %bitcast.5, f32[128,128]{1,0:T(8,128)} %constant.8.clone.cos_g_hbm, ...), custom_call_target="tpu_custom_call" | custom-call | flops 11000000512 | bytes 6000000 | tf_op jit(solution)/shard_map/pallas_call | solution.py:578
  64.9 1.6 %copy.15 = bf16[64,896]{1,0:T(8,128)(2,1)} copy(bf16[64,896]{1,0:T(8,128)(2,1)} %shard_map.127) | data formatting | bytes 229376
